TPU v7x, 32 devices: a whole 2x2x4 slice. The times are simulated.
32 devices in a mesh: dp: 4 (over y, x), expert: 8 (over z, core).
Axes of the slice: x: 2, y: 2, z: 4, core: 2. Of those that a mesh axis runs over, the one named last changes fastest.
Arguments:
- cotangent: bfloat16 [4096, 5120], P(('dp', 'expert')), may hold values from -6 to 6
- route_weights: float32 [4096, 6], P(('dp', 'expert')), may hold values from 0.05 to 1
- token_experts: int32 [4096, 6], P(('dp', 'expert')), may hold values from 0 to 159, as said below
- saved_hidden: bfloat16 [4, 8, 8, 16, 1536], P('dp', 'expert'), may hold values from -6 to 6
- previous_right: bfloat16 [8, 1536, 128], P('expert', 'dp'), may hold values from -8 to 8
Outputs:
- left_factor: float32 [8, 5120, 128], P('expert', 'dp')
- right_factor: float32 [8, 1536, 128], P('expert', 'dp')
Inputs may be any that keep to these rules, and one draw needn't show every extreme that they name: `token_experts`: each token names 6 different experts. On one device at most 16 tokens name any one of the experts 0 to 7, and in every draw one of these experts is named by exactly 16 tokens on every device.
All inputs are finite; a program needn't handle non-finite values.
Results may differ from a plain program's by a relative error of at most 0.0049.
Values may be sent and summed in bfloat16 or wider, within the bound.
No kernel may reach another device: no remote copies, remote signals or barrier semaphores. Data moves between devices by JAX's collectives and lax.ppermute only.
A program may use at most 64 MiB of HBM per device.

v0:
```python
import math

import jax
import jax.numpy as jnp
from jax import lax
from jax.sharding import PartitionSpec as P

EPSILON = 1e-06


def cholesky_pass(block):
    gram = jnp.dot(
        block.T, block, precision=lax.Precision.HIGHEST, preferred_element_type=jnp.float32
    )
    lower = jnp.linalg.cholesky(gram)
    orthogonal = lax.linalg.triangular_solve(
        lower, block, left_side=False, lower=True, transpose_a=True
    )
    return (orthogonal, lower.T)


def orthonormal(block):
    first, upper_one = cholesky_pass(block)
    second, upper_two = cholesky_pass(first)
    return (
        second,
        jnp.dot(
            upper_two,
            upper_one,
            precision=lax.Precision.HIGHEST,
            preferred_element_type=jnp.float32,
        ),
    )


def local(cotangent, route_weights, token_experts, saved_hidden, previous_right):
    window = lax.axis_size("expert")
    shards = lax.axis_size("dp")
    position = lax.axis_index("dp")
    token_count = cotangent.shape[0]
    model_width = cotangent.shape[1]
    capacity = saved_hidden.shape[3]
    hidden_width = saved_hidden.shape[4]
    contract_rows = (((0,), (0,)), ((), ()))
    expert_range = jnp.arange(window, dtype=jnp.int32)
    matches = token_experts[:, :, None] == expert_range[None, None, :]
    routed = jnp.any(matches, axis=1).astype(jnp.int32)
    weight_sum = jnp.sum(jnp.where(matches, route_weights[:, :, None], 0.0), axis=1)
    slots = jnp.cumsum(routed, axis=0) - routed
    chosen = (routed[:, :, None] == 1) & (
        slots[:, :, None] == jnp.arange(capacity, dtype=jnp.int32)[None, None, :]
    )
    token_range = jnp.arange(token_count, dtype=jnp.int32)
    source_row = jnp.sum(jnp.where(chosen, token_range[:, None, None], 0), axis=0)
    slot_weight = jnp.sum(jnp.where(chosen, weight_sum[:, :, None], 0.0), axis=0)
    picked = jnp.take(cotangent, source_row.reshape(-1), axis=0).reshape(
        window, capacity, model_width
    )
    outgoing = (picked * slot_weight[:, :, None]).astype(jnp.bfloat16)
    arrived = lax.all_to_all(outgoing, "expert", split_axis=0, concat_axis=0, tiled=True).reshape(
        window * capacity, model_width
    )
    hidden_rows = saved_hidden.reshape(window * capacity, hidden_width)
    right_whole = lax.all_gather(previous_right[0], "dp", axis=0, tiled=True)
    projected = jnp.dot(hidden_rows, right_whole, preferred_element_type=jnp.float32).astype(
        jnp.bfloat16
    )
    own_rows = model_width // shards
    gathered_left_terms = lax.dot_general(
        arrived, projected, contract_rows, preferred_element_type=jnp.float32
    )
    left_sum = lax.psum(gathered_left_terms, "dp")
    complete_basis_matrix, triangle = orthonormal(left_sum)
    basis = lax.dynamic_slice_in_dim(complete_basis_matrix, position * own_rows, own_rows, 0)
    rotated_factor = jnp.dot(
        arrived, complete_basis_matrix.astype(jnp.bfloat16), preferred_element_type=jnp.float32
    ).astype(jnp.bfloat16)
    right_own = lax.psum_scatter(
        lax.dot_general(
            hidden_rows, rotated_factor, contract_rows, preferred_element_type=jnp.float32
        ),
        "dp",
        scatter_dimension=0,
        tiled=True,
    )
    column_sums = lax.psum(jnp.sum(right_own * right_own, axis=0), "dp")
    right_out = right_own * (math.sqrt(hidden_width) / jnp.sqrt(column_sums + EPSILON))
    left_out = basis * math.sqrt(model_width)
    return (left_out[None], right_out[None])


def solution(mesh):
    in_specs = (
        P(("dp", "expert"), None),
        P(("dp", "expert"), None),
        P(("dp", "expert"), None),
        P("dp", "expert", None, None, None),
        P("expert", "dp", None),
    )
    out_specs = (P("expert", "dp", None), P("expert", "dp", None))
    return jax.shard_map(local, mesh=mesh, in_specs=in_specs, out_specs=out_specs, check_vma=False)
```

profile of v0, /device:TPU:0, one launch (start us, length us, event | category | flops | bytes accessed | tf_op | source)
XLA Modules:
  0.0 245.8 jit_solution(16574869929249323894)
XLA Ops:
  7.2 0.0 copy-start
  7.2 0.8 fusion.19
  8.0 0.1 copy.13
  8.1 0.2 reduce_window_sum.11
  8.4 0.1 copy.14
  8.4 0.2 select_reduce_fusion.2
  8.7 0.1 reshape.85
  8.8 0.7 select_reduce_fusion.3
  9.5 0.1 select_reduce_fusion.1
  9.6 0.0 copy-done
  9.6 1.3 gather_fusion
  10.9 0.0 copy-start.3
  10.9 0.0 copy-start.2
  11.0 1.5 multiply_convert_fusion
  12.4 6.3 %all-to-all-start = ((bf16[8,16,5120]{2,1,0:T(8,128)(2,1)}), bf16[8,16,5120]{2,1,0:T(8,128)(2,1)S(1)}, u32[]{:S(2)}, u32[]{:S(2)}) async-start(bf16[8,16,5120]{2,1,0:T(8,128)(2,1)} %multiply_convert_fusion), calls=%async_computation | async-start | bytes 2621440 | tf_op jit(solution)/shard_map/all_to_all | solution.py:60
  18.7 0.0 all-reduce.2.cloned.1.call-start
  18.8 0.0 copy-done.3
  18.8 9.6 %all-gather = bf16[1,1536,128]{2,1,0:T(8,128)(2,1)S(1)} all-gather(bf16[1,384,128]{2,1,0:T(8,128)(2,1)S(1)} %copy-done.3), channel_id=2, replica_groups=mesh['dp'=4,'expert'=8] {'dp'}, dimensions={1}, use_global_device_ids=true | all-gather | bytes 491520 | tf_op jit(solution)/shard_map/all_gather | solution.py:64
  28.4 22.6 %all-to-all-done = bf16[8,16,5120]{2,1,0:T(8,128)(2,1)S(1)} async-done(((bf16[8,16,5120]{2,1,0:T(8,128)(2,1)}), bf16[8,16,5120]{2,1,0:T(8,128)(2,1)S(1)}, u32[]{:S(2)}, u32[]{:S(2)}) %all-to-all-start) | async-done | bytes 1310752 | tf_op jit(solution)/shard_map/all_to_all | solution.py:60
  51.0 0.0 copy-done.2
  51.0 2.3 fusion.5
  53.2 0.0 all-reduce.2.cloned.1.call-update
  53.3 0.2 reduce-scatter.2.cloned.1.call-start
  53.5 77.3 %all-reduce.2.cloned.1.call-done = f32[5120,128]{1,0:T(8,128)} async-done(((f32[5120,128]{1,0:T(8,128)}), f32[5120,128]{1,0:T(8,128)}) %all-reduce.2.cloned.1.call-update) | async-done | bytes 2621456 | tf_op jit(solution)/shard_map/psum | solution.py:72
  130.8 6.8 %fusion.21 = f32[128,128]{1,0:T(8,128)S(1)} fusion(f32[5120,128]{1,0:T(8,128)} %all-reduce.2.cloned.1.call-done), kind=kOutput, calls=%fused_computation.46 | convolution fusion | flops 1006632960 | bytes 2686976 | tf_op jit(solution)/shard_map/dot_general | solution.py:12
  137.6 0.1 copy.16
  137.7 11.7 %cholesky.44 = f32[128,128]{1,0:T(8,128)S(1)} custom-call(f32[128,128]{1,0:T(8,128)S(1)} %fusion.15), custom_call_target="Cholesky" | custom-call | tf_op jit(solution)/shard_map/jit(cholesky)/cholesky | solution.py:15
  149.4 0.6 compare_reduce_fusion.1
  150.1 0.7 fusion.10
  150.7 9.8 %custom-call.6 = f32[1,128,128]{1,2,0:T(8,128)S(1)} custom-call(f32[1,128,128]{2,1,0:T(8,128)S(1)} %fusion.10), custom_call_target="InvertDiagBlocksLowerTriangular" | custom-call | tf_op jit(solution)/shard_map/triangular_solve/custom-call.0 | solution.py:16
  160.6 4.5 %convolution_bitcast_fusion.1 = f32[5120,128]{0,1:T(8,128)S(1)} fusion(f32[5120,128]{1,0:T(8,128)} %all-reduce.2.cloned.1.call-done, f32[1,128,128]{1,2,0:T(8,128)S(1)} %custom-call.6), kind=kOutput, calls=%fused_computation.2 | convolution fusion | flops 1006632960 | bytes 5308416 | tf_op jit(solution)/shard_map/triangular_solve/dot.4 | solution.py:16
  165.0 0.0 copy-start.1
  165.0 1.5 copy-done.1
  166.5 2.2 fusion.22
  168.7 0.1 copy.17
  168.9 11.7 %cholesky.55 = f32[128,128]{1,0:T(8,128)S(1)} custom-call(f32[128,128]{1,0:T(8,128)S(1)} %fusion.13), custom_call_target="Cholesky" | custom-call | tf_op jit(solution)/shard_map/jit(cholesky)/cholesky | solution.py:15
  180.6 0.6 compare_reduce_fusion
  181.2 0.7 fusion.11
  181.9 9.8 %custom-call.7 = f32[1,128,128]{1,2,0:T(8,128)S(1)} custom-call(f32[1,128,128]{2,1,0:T(8,128)S(1)} %fusion.11), custom_call_target="InvertDiagBlocksLowerTriangular" | custom-call | tf_op jit(solution)/shard_map/triangular_solve/custom-call.0 | solution.py:16
  191.7 5.6 %convolution_bitcast_fusion = f32[5120,128]{0,1:T(8,128)} fusion(f32[5120,128]{0,1:T(8,128)} %copy-done.1, f32[1,128,128]{1,2,0:T(8,128)S(1)} %custom-call.7), kind=kOutput, calls=%fused_computation.1 | convolution fusion | flops 1006632960 | bytes 5308416 | tf_op jit(solution)/shard_map/triangular_solve/dot.4 | solution.py:16
  197.3 3.6 %convolution_bitcast_fusion.2 = f32[1536,128]{0,1:T(8,128)} fusion(bf16[128,1536]{1,0:T(8,128)(2,1)S(1)} %bitcast.51, bf16[128,5120]{1,0:T(8,128)(2,1)S(1)} %bitcast.48, f32[5120,128]{0,1:T(8,128)} %convolution_bitcast_fusion), kind=kOutput, calls=%fused_computation.4 | convolution fusion | flops 218775552 | bytes 5111808 | tf_op jit(solution)/shard_map/dot_general | solution.py:79
  200.9 0.0 reduce-scatter.2.cloned.1.call-update
  200.9 1.2 multiply_bitcast_fusion
  202.1 1.1 copy.18
  203.2 24.0 %reduce-scatter.2.cloned.1.call-done = f32[384,128]{0,1:T(8,128)} async-done(((f32[1536,128]{0,1:T(8,128)}), f32[384,128]{0,1:T(8,128)}) %reduce-scatter.2.cloned.1.call-update) | async-done | bytes 196624 | tf_op jit(solution)/shard_map/reduce_scatter | solution.py:78
  227.2 1.0 multiply_reduce_fusion
  228.2 8.9 %psum.15 = f32[128]{0:T(128)S(1)} all-reduce(f32[128]{0:T(128)S(1)} %multiply_reduce_fusion), channel_id=1, replica_groups=mesh['dp'=4,'expert'=8] {'dp'}, use_global_device_ids=true, to_apply=%region_10.13 | all-reduce | flops 128 | bytes 1024 | tf_op jit(solution)/shard_map/psum | solution.py:86
  237.1 1.0 multiply_bitcast_fusion.1
  238.2 0.8 copy.19
  (11 shorter events, 0.2 us)
Async XLA Ops:
  7.2 2.5 copy-start
  10.9 7.9 %copy-start.3 = (bf16[1,384,128]{2,1,0:T(8,128)(2,1)S(1)}, bf16[1,384,128]{2,1,0:T(8,128)(2,1)}, u32[]{:S(2)}) copy-start(bf16[1,384,128]{2,1,0:T(8,128)(2,1)} %param.12) | copy-start | bytes 294916
  10.9 40.0 %copy-start.2 = (bf16[1,1,8,16,1536]{4,3,2,1,0:T(8,128)(2,1)S(1)}, bf16[1,1,8,16,1536]{4,3,2,1,0:T(8,128)(2,1)}, u32[]{:S(2)}) copy-start(bf16[1,1,8,16,1536]{4,3,2,1,0:T(8,128)(2,1)} %param.11) | copy-start | bytes 1179652
  12.4 38.5 %all-to-all-start = ((bf16[8,16,5120]{2,1,0:T(8,128)(2,1)}), bf16[8,16,5120]{2,1,0:T(8,128)(2,1)S(1)}, u32[]{:S(2)}, u32[]{:S(2)}) async-start(bf16[8,16,5120]{2,1,0:T(8,128)(2,1)} %multiply_convert_fusion), calls=%async_computation | async-start | bytes 2621440 | tf_op jit(solution)/shard_map/all_to_all | solution.py:60
  18.7 112.0 %all-reduce.2.cloned.1.call-start = ((), (), s32[]{:S(2)}) async-start(), calls=%async_computation.2 | async-start | bytes 5242880 | tf_op jit(solution)/shard_map/psum | solution.py:72
  53.3 173.9 %reduce-scatter.2.cloned.1.call-start = ((), (), s32[]{:S(2)}) async-start(), calls=%async_computation.3 | async-start | bytes 983040 | tf_op jit(solution)/shard_map/reduce_scatter | solution.py:78
  165.0 1.5 copy-start.1
Sparse Core Ops, SparseCore 0:
  53.4 77.3 all-reduce.1
  201.1 26.0 reduce-scatter.1
where the time goes:
time: 246 us
  waiting for transfers between devices  124 us (50%)
  other arithmetic  52.5 us (21%)
  matrix products  24.9 us (10%)
  blocking collectives  18.5 us (8%)
  between operations  14.2 us (6%)
  starting transfers between devices  6.58 us (3%)
  local copies, waits for them, and re-layouts  5.24 us (2%)
    psum x1, waiting for transfers between devices, local(): left_sum = lax.psum(gathered_left_terms, 'dp')  77.3 us
    another operation x6, other arithmetic, cholesky_pass(): lower = jnp.linalg.cholesky(gram)  24.8 us
    reduce_scatter x1, waiting for transfers between devices, local(): lax.psum_scatter(lax.dot_general(hidden_rows, rotated_factor, contract_ro...  24 us
    all_to_all x1, waiting for transfers between devices, local(): lax.all_to_all(outgoing, 'expert', split_axis=0, concat_axis=0, tiled=True)  22.6 us
    another operation x4, other arithmetic, cholesky_pass(): lax.linalg.triangular_solve(lower, block, left_side=False, lower=True, tr...  20.9 us
    another operation x2, matrix products, cholesky_pass(): lax.linalg.triangular_solve(lower, block, left_side=False, lower=True, tr...  10 us
    all_gather x1, blocking collectives, local(): right_whole = lax.all_gather(previous_right[0], 'dp', axis=0, tiled=True)  9.58 us
    dot_general x2, matrix products, cholesky_pass(): jnp.dot(block.T, block, precision=lax.Precision.HIGHEST, preferred_elemen...  8.99 us
  transfers between devices with their start and end apart: 3, of which 3 were waited for; matrix products, arithmetic and copies ran while one was open for 1% of the time, Pallas kernels for 0%

commit v1 on v0

v1 whole, which is shorter than its diff:
```python
import math

import jax
import jax.numpy as jnp
from jax import lax
from jax.sharding import PartitionSpec as P

EPSILON = 1e-06
HIGHEST = lax.Precision.HIGHEST
CONTRACT_ROWS = (((0,), (0,)), ((), ()))


def inverse_upper(gram):
    lower = jnp.linalg.cholesky(gram)
    identity = jnp.eye(gram.shape[0], dtype=jnp.float32)
    return lax.linalg.triangular_solve(
        lower, identity, left_side=False, lower=True, transpose_a=True
    )


def sum_over_dp(value, shards):
    step = 1
    while step < shards:
        other = lax.ppermute(value, "dp", [(i, i ^ step) for i in range(shards)])
        value = value + other
        step *= 2
    return value


def local(cotangent, route_weights, token_experts, saved_hidden, previous_right):
    window = lax.axis_size("expert")
    shards = lax.axis_size("dp")
    position = lax.axis_index("dp")
    token_count, model_width = cotangent.shape
    capacity = saved_hidden.shape[3]
    hidden_width = saved_hidden.shape[4]
    own_columns = model_width // shards
    own_hidden = hidden_width // shards

    hidden_rows = lax.all_gather(
        saved_hidden.reshape(window * capacity, hidden_width), "dp", axis=0, tiled=True
    )
    right_whole = lax.all_gather(previous_right[0], "dp", axis=0, tiled=True)

    expert_range = jnp.arange(window, dtype=jnp.int32)
    matches = token_experts[:, :, None] == expert_range[None, None, :]
    routed = jnp.any(matches, axis=1).astype(jnp.int32)
    weight_sum = jnp.sum(jnp.where(matches, route_weights[:, :, None], 0.0), axis=1)
    slots = jnp.cumsum(routed, axis=0) - routed
    chosen = (routed[:, :, None] == 1) & (
        slots[:, :, None] == jnp.arange(capacity, dtype=jnp.int32)[None, None, :]
    )
    token_range = jnp.arange(token_count, dtype=jnp.int32)
    source_row = jnp.sum(jnp.where(chosen, token_range[:, None, None], 0), axis=0)
    slot_weight = jnp.sum(jnp.where(chosen, weight_sum[:, :, None], 0.0), axis=0)
    picked = jnp.take(cotangent, source_row.reshape(-1), axis=0).reshape(
        window * capacity, shards, own_columns
    )
    outgoing = (picked * slot_weight.reshape(-1)[:, None, None]).astype(jnp.bfloat16)
    outgoing = outgoing.transpose(1, 0, 2).reshape(shards * window, capacity, own_columns)
    arrived = lax.all_to_all(
        outgoing, ("dp", "expert"), split_axis=0, concat_axis=0, tiled=True
    ).reshape(shards * window * capacity, own_columns)

    projected = (
        jnp.dot(hidden_rows, right_whole, preferred_element_type=jnp.float32)
        .astype(jnp.bfloat16)
        .astype(jnp.float32)
    )
    inner = inverse_upper(
        lax.dot_general(
            projected, projected, CONTRACT_ROWS, precision=HIGHEST,
            preferred_element_type=jnp.float32,
        )
    )
    prepared = jnp.dot(projected, inner, precision=HIGHEST, preferred_element_type=jnp.float32)

    rows = arrived.astype(jnp.float32)
    left_part = lax.dot_general(
        rows, prepared, CONTRACT_ROWS, precision=HIGHEST, preferred_element_type=jnp.float32
    )
    gram = lax.dot_general(
        left_part, left_part, CONTRACT_ROWS, precision=HIGHEST,
        preferred_element_type=jnp.float32,
    )
    turned = jnp.dot(rows, left_part, precision=HIGHEST, preferred_element_type=jnp.float32)
    gram = sum_over_dp(gram, shards)
    turned = sum_over_dp(turned, shards)
    outer = inverse_upper(gram)
    left_out = jnp.dot(
        left_part, outer * math.sqrt(model_width), precision=HIGHEST,
        preferred_element_type=jnp.float32,
    )
    rotated = jnp.dot(turned, outer, precision=HIGHEST, preferred_element_type=jnp.float32)
    right_sum = lax.dot_general(
        hidden_rows.astype(jnp.float32), rotated, CONTRACT_ROWS, precision=HIGHEST,
        preferred_element_type=jnp.float32,
    )
    column_sums = jnp.sum(right_sum * right_sum, axis=0)
    right_own = lax.dynamic_slice_in_dim(right_sum, position * own_hidden, own_hidden, 0)
    right_out = right_own * (math.sqrt(hidden_width) / jnp.sqrt(column_sums + EPSILON))
    return (left_out[None], right_out[None])


def solution(mesh):
    in_specs = (
        P(("dp", "expert"), None),
        P(("dp", "expert"), None),
        P(("dp", "expert"), None),
        P("dp", "expert", None, None, None),
        P("expert", "dp", None),
    )
    out_specs = (P("expert", "dp", None), P("expert", "dp", None))
    return jax.shard_map(local, mesh=mesh, in_specs=in_specs, out_specs=out_specs, check_vma=False)
```

time: 246 us -> 134 us (0.54)
  waiting for transfers between devices: 124 us -> 22.5 us
  matrix products: 24.9 us -> 9.78 us
  starting transfers between devices: 6.58 us -> 11.8 us
  blocking collectives: 18.5 us -> 23.2 us
  other arithmetic: 52.5 us -> 49.5 us
    psum x1 -> x0, waiting for transfers between devices: 77.3 us -> none  [local(): left_sum = lax.psum(gathered_left_terms, 'dp')]
    reduce_scatter x1 -> x0, waiting for transfers between devices: 24 us -> none  [local(): lax.psum_scatter(lax.dot_general(hidden_rows, rotated_factor, contract_ro...]
    all_to_all x1, waiting for transfers between devices: 22.6 us -> 0.01 us  [local(): lax.all_to_all(outgoing, ('dp', 'expert'), split_axis=0, concat_axis=0, t...]
    all_gather x0 -> x1, waiting for transfers between devices: none -> 14.2 us  [local(): lax.all_gather(saved_hidden.reshape(window * capacity, hidden_width), 'dp...]
    all_gather x1, blocking collectives: 9.58 us -> 23.2 us  [local(): right_whole = lax.all_gather(previous_right[0], 'dp', axis=0, tiled=True)]
    another operation x2, matrix products: 10 us -> 0.57 us  [inverse_upper(): lax.linalg.triangular_solve(lower, identity, left_side=False, lower=True,...]
    psum x1 -> x0, blocking collectives: 8.92 us -> none  [local(): column_sums = lax.psum(jnp.sum(right_own * right_own, axis=0), 'dp')]
    ppermute x0 -> x4, waiting for transfers between devices: none -> 7.58 us  [sum_over_dp(): other = lax.ppermute(value, 'dp', [(i, i ^ step) for i in range(shards)])]
  transfers between devices with their start and end apart: 3 -> 6, of which waited for: 3 -> 4; matrix products, arithmetic and copies ran while one was open for 1% -> 43% of each run, Pallas kernels for 0% -> 0%
where the time goes in v1:
time: 134 us
  other arithmetic  49.5 us (37%)
  blocking collectives  23.2 us (17%)
  waiting for transfers between devices  22.5 us (17%)
  between operations  14.3 us (11%)
  starting transfers between devices  11.8 us (9%)
  matrix products  9.78 us (7%)
  local copies, waits for them, and re-layouts  2.81 us (2%)
    another operation x6, other arithmetic, inverse_upper(): lower = jnp.linalg.cholesky(gram)  24.9 us
    all_gather x1, blocking collectives, local(): right_whole = lax.all_gather(previous_right[0], 'dp', axis=0, tiled=True)  23.2 us
    another operation x4, other arithmetic, inverse_upper(): lax.linalg.triangular_solve(lower, identity, left_side=False, lower=True,...  20.9 us
    all_gather x1, waiting for transfers between devices, local(): lax.all_gather(saved_hidden.reshape(window * capacity, hidden_width), 'dp...  14.2 us
    ppermute x4, waiting for transfers between devices, sum_over_dp(): other = lax.ppermute(value, 'dp', [(i, i ^ step) for i in range(shards)])  7.58 us
    all_to_all x1, starting transfers between devices, local(): lax.all_to_all(outgoing, ('dp', 'expert'), split_axis=0, concat_axis=0, t...  7.3 us
    ppermute x4, starting transfers between devices, sum_over_dp(): other = lax.ppermute(value, 'dp', [(i, i ^ step) for i in range(shards)])  4.49 us
  transfers between devices with their start and end apart: 6, of which 4 were waited for; matrix products, arithmetic and copies ran while one was open for 43% of the time, Pallas kernels for 0%

profile of v1, /device:TPU:0, one launch (start us, length us, event | category | flops | bytes accessed | tf_op | source)
XLA Modules:
  0.0 133.9 jit_solution(9777394413942327370)
XLA Ops:
  7.2 0.0 copy-start
  7.2 0.0 all-gather.3.cloned.1.call-start
  7.2 0.7 all-gather.3.cloned.1.call-update
  7.9 0.7 fusion.14
  8.6 0.1 copy.22
  8.8 0.2 reduce_window_sum.11
  9.0 0.1 copy.23
  9.1 0.2 select_reduce_fusion.3
  9.3 0.1 reshape.95
  9.4 0.1 reshape.94
  9.5 0.7 select_reduce_fusion.4
  10.2 0.1 select_reduce_fusion.2
  10.3 0.1 mul.34
  10.4 0.0 copy-done
  10.4 1.3 gather_fusion
  11.7 1.5 %multiply_convert_fusion = bf16[128,4,1280]{2,0,1:T(8,128)(2,1)} fusion(bf16[16,4,8,1280]{3,2,1,0:T(8,128)(2,1)S(1)} %bitcast.60, f32[128]{0:T(128)S(1)} %mul.34, pred[128]{0:T(512)(128)(4,1)S(1)} %compare_and_fusion), kind=kLoop, calls=%fused_computation.1 | loop fusion | flops 2621440 | bytes 2622080 | tf_op jit(solution)/shard_map/convert_element_type | solution.py:59
  13.2 0.0 copy-start.2
  13.2 7.3 %all-to-all-start = ((bf16[32,16,1280]{2,1,0:T(8,128)(2,1)}), bf16[32,16,1280]{2,1,0:T(8,128)(2,1)S(1)}, u32[]{:S(2)}, u32[]{:S(2)}) async-start(bf16[32,16,1280]{2,1,0:T(8,128)(2,1)} %bitcast.61), calls=%async_computation | async-start | bytes 2621440 | tf_op jit(solution)/shard_map/all_to_all | solution.py:61
  20.5 0.0 copy-done.2
  20.5 23.2 %all-gather = bf16[1,1536,128]{2,1,0:T(8,128)(2,1)S(1)} all-gather(bf16[1,384,128]{2,1,0:T(8,128)(2,1)S(1)} %copy-done.2), channel_id=2, replica_groups=mesh['dp'=4,'expert'=8] {'dp'}, dimensions={1}, use_global_device_ids=true | all-gather | bytes 491520 | tf_op jit(solution)/shard_map/all_gather | solution.py:43
  43.7 14.2 %all-gather.3.cloned.1.call-done = bf16[512,1536]{1,0:T(8,128)(2,1)} async-done(((bf16[128,1536]{1,0:T(8,128)(2,1)}), bf16[512,1536]{1,0:T(8,128)(2,1)}) %all-gather.3.cloned.1.call-update) | async-done | bytes 1572880 | tf_op jit(solution)/shard_map/all_gather | solution.py:40
  57.9 2.0 %convolution_convert_fusion = bf16[512,128]{1,0:T(8,128)(2,1)S(1)} fusion(bf16[512,1536]{1,0:T(8,128)(2,1)} %all-gather.3.cloned.1.call-done, bf16[1,1536,128]{2,1,0:T(8,128)(2,1)S(1)} %all-gather), kind=kOutput, calls=%fused_computation.4 | convolution fusion | flops 201392128 | bytes 2097152 | tf_op jit(solution)/shard_map/dot_general | solution.py:66
  59.9 0.2 fusion.17
  60.1 0.1 copy.26
  60.3 11.7 %cholesky.44 = f32[128,128]{1,0:T(8,128)S(1)} custom-call(f32[128,128]{1,0:T(8,128)S(1)} %fusion.10), custom_call_target="Cholesky" | custom-call | tf_op jit(solution)/shard_map/jit(cholesky)/cholesky | solution.py:14
  72.0 0.6 compare_reduce_fusion.1
  72.7 0.7 fusion.5
  73.3 9.8 %custom-call.6 = f32[1,128,128]{1,2,0:T(8,128)S(1)} custom-call(f32[1,128,128]{2,1,0:T(8,128)S(1)} %fusion.5), custom_call_target="InvertDiagBlocksLowerTriangular" | custom-call | tf_op jit(solution)/shard_map/triangular_solve/custom-call.0 | solution.py:16
  83.1 0.3 convolution_bitcast_fusion.2
  83.4 0.3 fusion.18
  83.7 0.0 all-to-all-done
  83.7 1.5 %fusion.19 = f32[1280,128]{1,0:T(8,128)S(1)} fusion(bf16[512,1280]{1,0:T(8,128)(2,1)S(1)} %bitcast.58, f32[512,128]{1,0:T(8,128)S(1)} %fusion.18), kind=kOutput, calls=%fused_computation.50 | convolution fusion | flops 1006632960 | bytes 2228224 | tf_op jit(solution)/shard_map/dot_general | solution.py:79
  85.2 1.2 fusion.20
  86.4 0.8 collective-permute-start
  87.2 3.5 %collective-permute-done = f32[128,128]{0,1:T(8,128)S(1)} collective-permute-done((f32[128,128]{0,1:T(8,128)S(1)}, f32[128,128]{0,1:T(8,128)S(1)}, u32[]{:S(2)}, u32[]{:S(2)}) %collective-permute-start) | collective-permute-done | bytes 65568 | tf_op jit(solution)/shard_map/ppermute | solution.py:24
  90.8 1.5 %collective-permute-start.1 = (f32[128,128]{0,1:T(8,128)S(1)}, f32[128,128]{0,1:T(8,128)S(1)}, u32[]{:S(2)}, u32[]{:S(2)}) collective-permute-start(f32[128,128]{0,1:T(8,128)S(1)} %add.58), channel_id=1, source_target_pairs={{0,16},{8,24},{16,0},{24,8},{1,17},{9,25},{17,1},{25,9},{2,18},{10... | collective-permute-start | bytes 196616 | tf_op jit(solution)/shard_map/ppermute | solution.py:24
  92.3 1.2 fusion.21
  93.5 0.6 collective-permute-start.2
  94.1 1.0 collective-permute-done.1
  95.1 0.1 copy.29
  95.2 11.9 %cholesky.55 = f32[128,128]{1,0:T(8,128)S(1)} custom-call(f32[128,128]{1,0:T(8,128)S(1)} %fusion.8), custom_call_target="Cholesky" | custom-call | tf_op jit(solution)/shard_map/jit(cholesky)/cholesky | solution.py:14
  107.1 0.6 compare_reduce_fusion
  107.8 0.7 fusion.6
  108.5 9.8 %custom-call.7 = f32[1,128,128]{1,2,0:T(8,128)S(1)} custom-call(f32[1,128,128]{2,1,0:T(8,128)S(1)} %fusion.6), custom_call_target="InvertDiagBlocksLowerTriangular" | custom-call | tf_op jit(solution)/shard_map/triangular_solve/custom-call.0 | solution.py:16
  118.3 0.0 collective-permute-done.2
  118.3 0.0 copy-start.1
  118.3 1.5 %collective-permute-start.3 = (f32[512,128]{1,0:T(8,128)S(1)}, f32[512,128]{1,0:T(8,128)S(1)}, u32[]{:S(2)}, u32[]{:S(2)}) collective-permute-start(f32[512,128]{1,0:T(8,128)S(1)} %add.60), channel_id=1, source_target_pairs={{0,16},{8,24},{16,0},{24,8},{1,17},{9,25},{17,1},{25,9},{2,18},{10... | collective-permute-start | bytes 786440 | tf_op jit(solution)/shard_map/ppermute | solution.py:24
  119.9 0.3 convolution_bitcast_fusion.1
  120.2 1.5 %convolution_bitcast_fusion = f32[1,1280,128]{2,1,0:T(8,128)} fusion(f32[1280,128]{1,0:T(8,128)S(1)} %fusion.19, f32[128,128]{0,1:T(8,128)S(1)} %convolution_bitcast_fusion.1), kind=kOutput, calls=%fused_computation.2 | convolution fusion | flops 251674624 | bytes 1376256 | tf_op jit(solution)/shard_map/dot_general | solution.py:90
  121.7 3.1 %collective-permute-done.3 = f32[512,128]{1,0:T(8,128)S(1)} collective-permute-done((f32[512,128]{1,0:T(8,128)S(1)}, f32[512,128]{1,0:T(8,128)S(1)}, u32[]{:S(2)}, u32[]{:S(2)}) %collective-permute-start.3) | collective-permute-done | bytes 262176 | tf_op jit(solution)/shard_map/ppermute | solution.py:24
  124.8 0.4 fusion.1
  125.1 0.0 copy-done.1
  125.2 0.9 multiply_reduce_fusion
  126.1 0.1 multiply_bitcast_fusion
  126.2 0.8 copy.30
  (14 shorter events, 0.2 us)
Async XLA Ops:
  7.2 3.2 %copy-start = (bf16[128,5120]{1,0:T(8,128)(2,1)S(1)}, bf16[128,5120]{1,0:T(8,128)(2,1)}, u32[]{:S(2)}) copy-start(bf16[128,5120]{1,0:T(8,128)(2,1)} %param.8) | copy-start | bytes 3932164
  7.2 50.8 %all-gather.3.cloned.1.call-start = ((), (), s32[]{:S(2)}) async-start(), calls=%async_computation.1 | async-start | bytes 1966080 | tf_op jit(solution)/shard_map/all_gather | solution.py:40
  13.2 7.3 %copy-start.2 = (bf16[1,384,128]{2,1,0:T(8,128)(2,1)S(1)}, bf16[1,384,128]{2,1,0:T(8,128)(2,1)}, u32[]{:S(2)}) copy-start(bf16[1,384,128]{2,1,0:T(8,128)(2,1)} %param.12) | copy-start | bytes 294916
  13.2 70.5 %all-to-all-start = ((bf16[32,16,1280]{2,1,0:T(8,128)(2,1)}), bf16[32,16,1280]{2,1,0:T(8,128)(2,1)S(1)}, u32[]{:S(2)}, u32[]{:S(2)}) async-start(bf16[32,16,1280]{2,1,0:T(8,128)(2,1)} %bitcast.61), calls=%async_computation | async-start | bytes 2621440 | tf_op jit(solution)/shard_map/all_to_all | solution.py:61
  86.4 4.3 %collective-permute-start = (f32[128,128]{0,1:T(8,128)S(1)}, f32[128,128]{0,1:T(8,128)S(1)}, u32[]{:S(2)}, u32[]{:S(2)}) collective-permute-start(f32[128,128]{0,1:T(8,128)S(1)} %fusion.20), channel_id=1, source_target_pairs={{0,8},{8,0},{16,24},{24,16},{1,9},{9,1},{17,25},{25,17},{2,10},{10... | collective-permute-start | bytes 196616 | tf_op jit(solution)/shard_map/ppermute | solution.py:24
  90.8 4.3 %collective-permute-start.1 = (f32[128,128]{0,1:T(8,128)S(1)}, f32[128,128]{0,1:T(8,128)S(1)}, u32[]{:S(2)}, u32[]{:S(2)}) collective-permute-start(f32[128,128]{0,1:T(8,128)S(1)} %add.58), channel_id=1, source_target_pairs={{0,16},{8,24},{16,0},{24,8},{1,17},{9,25},{17,1},{25,9},{2,18},{10... | collective-permute-start | bytes 196616 | tf_op jit(solution)/shard_map/ppermute | solution.py:24
  93.5 24.7 %collective-permute-start.2 = (f32[512,128]{1,0:T(8,128)S(1)}, f32[512,128]{1,0:T(8,128)S(1)}, u32[]{:S(2)}, u32[]{:S(2)}) collective-permute-start(f32[512,128]{1,0:T(8,128)S(1)} %fusion.21), channel_id=1, source_target_pairs={{0,8},{8,0},{16,24},{24,16},{1,9},{9,1},{17,25},{25,17},{2,10},{10... | collective-permute-start | bytes 786440 | tf_op jit(solution)/shard_map/ppermute | solution.py:24
  118.3 6.8 %copy-start.1 = (bf16[512,1536]{1,0:T(8,128)(2,1)S(1)}, bf16[512,1536]{1,0:T(8,128)(2,1)}, u32[]{:S(2)}) copy-start(bf16[512,1536]{1,0:T(8,128)(2,1)} %all-gather.3.cloned.1.call-done) | copy-start | bytes 4718596
  118.3 6.4 %collective-permute-start.3 = (f32[512,128]{1,0:T(8,128)S(1)}, f32[512,128]{1,0:T(8,128)S(1)}, u32[]{:S(2)}, u32[]{:S(2)}) collective-permute-start(f32[512,128]{1,0:T(8,128)S(1)} %add.60), channel_id=1, source_target_pairs={{0,16},{8,24},{16,0},{24,8},{1,17},{9,25},{17,1},{25,9},{2,18},{10... | collective-permute-start | bytes 786440 | tf_op jit(solution)/shard_map/ppermute | solution.py:24
Sparse Core Ops, SparseCore 0:
  9.9 48.0 all-gather.2
